TPU v7x, 512 devices: a whole 4x8x8 slice. The times are simulated.
512 devices in a mesh: dp: 64 (over z_hi, y, core), tensor: 8 (over z_lo, x).
Axes of the slice: x: 4, y: 8, z: 8 (z_hi: 4, z_lo: 2; z = z_hi * 2 + z_lo), core: 2. Of those that a mesh axis runs over, the one named last changes fastest.
Arguments:
- tokens: bfloat16 [32768, 8192], P('dp', 'tensor'), may hold values from -6 to 6
- value_weight: bfloat16 [8192, 1024], P('tensor', 'dp'), may hold values from -0.0625 to 0.0625
- adapter_down_weights: bfloat16 [8, 8192, 64], P(None, 'tensor'), may hold values from -0.0625 to 0.0625
- adapter_up_weights: bfloat16 [8, 64, 1024], P(None, None, 'tensor'), may hold values from -0.75 to 0.75
- value_gradient: bfloat16 [32768, 1024], P(('dp', 'tensor')), may hold values from -12 to 12
- block_adapter_index: int32 [256, 1], replicated, may hold values from 0 to 7
- block_live_rows: int32 [256], replicated, may hold values from 1 to 128
Outputs:
- values_out: bfloat16 [32768, 1024], P(('dp', 'tensor'))
- input_gradient: bfloat16 [32768, 8192], P('dp', 'tensor')
- grad_a: float32 [8, 8192, 64], P(None, 'tensor')
- grad_b: float32 [8, 64, 1024], P(None, None, 'tensor')
Inputs may be any that keep to these rules, and one draw needn't show every extreme that they name: `block_adapter_index`: every adapter names at least one block.
All inputs are finite; a program needn't handle non-finite values.
Results may differ from a plain program's by a relative error of at most 0.02.
Values may be sent and summed in bfloat16 or wider, within the bound.
No kernel may reach another device: no remote copies, remote signals or barrier semaphores. Data moves between devices by JAX's collectives and lax.ppermute only.
A program may use at most 64 MiB of HBM per device.

v0:
```python
import jax
import jax.numpy as jnp
from jax import lax
from jax.sharding import PartitionSpec as P

BLK = 128
ADAPTER_SCALE = 2.0


def shards(
    tokens,
    value_weight,
    adapter_down_weights,
    adapter_up_weights,
    value_gradient,
    block_adapter_index,
    block_live_rows,
):
    local_rows = tokens.shape[0]
    tensor_size = lax.axis_size("tensor")
    own_rows = local_rows // tensor_size
    data_index = lax.axis_index("dp")
    tensor_index = lax.axis_index("tensor")
    adapter_count = adapter_down_weights.shape[0]
    local_width = tokens.shape[1]
    rank_columns = adapter_down_weights.shape[2]
    head_columns = adapter_up_weights.shape[2]
    local_blocks = local_rows // BLK
    all_ids = block_adapter_index[:, 0]
    block_indices = lax.dynamic_slice_in_dim(all_ids, data_index * local_blocks, local_blocks)
    block_fill = lax.dynamic_slice_in_dim(block_live_rows, data_index * local_blocks, local_blocks)
    adapter_range = jnp.arange(adapter_count, dtype=jnp.int32)
    block_onehot = (block_indices[:, None] == adapter_range[None, :]).astype(jnp.float32)
    complete_up_weight = lax.all_gather(adapter_up_weights, "tensor", axis=2, tiled=True)
    up_flat = complete_up_weight.reshape(adapter_count * rank_columns, complete_up_weight.shape[2])
    selected_down_weight = adapter_down_weights[block_indices]
    token_block_rows = tokens.reshape(local_blocks, BLK, local_width)
    reduced_part = jnp.einsum(
        "cpe,cev->cpv", token_block_rows, selected_down_weight, preferred_element_type=jnp.float32
    )
    reduced = lax.psum(reduced_part.astype(jnp.bfloat16), "tensor")
    w_full = lax.all_gather(value_weight, "dp", axis=1, tiled=True)
    base_own = lax.psum_scatter(
        jnp.dot(tokens, w_full, preferred_element_type=jnp.float32).astype(jnp.bfloat16),
        "tensor",
        scatter_dimension=0,
        tiled=True,
    ).astype(jnp.float32)
    row_index = tensor_index * own_rows + jnp.arange(own_rows, dtype=jnp.int32)
    row_block = row_index // BLK
    row_ids = block_indices[row_block]
    row_onehot = row_ids[:, None] == adapter_range[None, :]
    reduced_own = lax.dynamic_slice_in_dim(
        reduced.reshape(local_rows, rank_columns), tensor_index * own_rows, own_rows, 0
    )
    spread = (row_onehot[:, :, None].astype(jnp.bfloat16) * reduced_own[:, None, :]).reshape(
        own_rows, adapter_count * rank_columns
    )
    update = jnp.dot(spread, up_flat, preferred_element_type=jnp.float32)
    values_out = (base_own + ADAPTER_SCALE * update).astype(jnp.bfloat16)
    live_rows = row_index % BLK < block_fill[row_block]
    masked = jnp.where(live_rows[:, None], value_gradient, jnp.zeros_like(value_gradient))
    projected = jnp.einsum("kc,mc->km", masked, up_flat, preferred_element_type=jnp.float32)
    grad_low = jnp.sum(
        projected.reshape(own_rows, adapter_count, rank_columns)
        * row_onehot[:, :, None].astype(jnp.float32),
        axis=1,
    ).astype(jnp.bfloat16)
    whole_grad, whole_low = (
        lax.all_gather(masked, "tensor", axis=0, tiled=True),
        lax.all_gather(grad_low, "tensor", axis=0, tiled=True),
    )
    lowrank_block_rows = whole_low.reshape(local_blocks, BLK, rank_columns)
    base_backward = jnp.einsum("kc,dc->kd", whole_grad, w_full, preferred_element_type=jnp.float32)
    adapter_backward = jnp.einsum(
        "sly,say->sla", lowrank_block_rows, selected_down_weight, preferred_element_type=jnp.float32
    ).reshape(local_rows, local_width)
    input_gradient = (base_backward + ADAPTER_SCALE * adapter_backward).astype(jnp.bfloat16)
    down_terms = jnp.einsum(
        "xgj,xgi->xji", token_block_rows, lowrank_block_rows, preferred_element_type=jnp.float32
    )
    down_local = jnp.einsum(
        "ba,bdr->adr", block_onehot, down_terms, precision=lax.Precision.HIGHEST
    )
    grad_cols = lax.dynamic_slice_in_dim(
        whole_grad, tensor_index * head_columns, head_columns, 1
    ).reshape(local_blocks, BLK, head_columns)
    up_terms = jnp.einsum("bkr,bkc->brc", reduced, grad_cols, preferred_element_type=jnp.float32)
    up_local = jnp.einsum("ba,brc->arc", block_onehot, up_terms, precision=lax.Precision.HIGHEST)
    all_onehot = (all_ids[:, None] == adapter_range[None, :]).astype(jnp.float32)
    tallies = jnp.sum(all_onehot * block_live_rows[:, None].astype(jnp.float32), axis=0)
    factor = ADAPTER_SCALE / tallies
    down_sum, up_sum = lax.psum((down_local, up_local), "dp")
    grad_a = down_sum * factor[:, None, None]
    grad_b = up_sum * factor[:, None, None]
    return (values_out, input_gradient, grad_a, grad_b)


def solution(mesh):
    return jax.shard_map(
        shards,
        mesh=mesh,
        in_specs=(
            P("dp", "tensor"),
            P("tensor", "dp"),
            P(None, "tensor", None),
            P(None, None, "tensor"),
            P(("dp", "tensor"), None),
            P(),
            P(),
        ),
        out_specs=(
            P(("dp", "tensor"), None),
            P("dp", "tensor"),
            P(None, "tensor", None),
            P(None, None, "tensor"),
        ),
        check_vma=False,
    )
```

profile of v0, /device:TPU:8, one launch (start us, length us, event | category | flops | bytes accessed | tf_op | source)
XLA Modules:
  0.0 890.9 jit_solution(14993300499443759841)
XLA Ops:
  7.2 0.0 copy-start
  7.2 0.0 all-gather.6.cloned.1.call-start
  7.2 0.7 all-gather.6.cloned.1.call-update
  7.9 0.0 all-gather.8.cloned.1.call-start
  8.0 0.8 dynamic_slice.17
  8.7 0.6 fusion.26
  9.3 2.6 fusion.21
  11.9 1.6 broadcast_select_fusion
  13.6 0.0 all-gather.8.cloned.1.call-update
  13.6 0.0 all-reduce.4.cloned.1.call-start
  13.6 0.7 fusion.25
  14.4 1.8 gather_fusion
  16.2 1.1 fusion.5
  17.3 0.0 all-reduce.4.cloned.1.call-update
  17.3 0.0 all-gather.4.cloned.1.call-start
  17.4 0.5 all-gather.4.cloned.1.call-update
  17.9 0.0 all-reduce.6.cloned.1.call-start
  18.0 0.6 fusion.27
  18.6 2.6 fusion.23
  21.2 36.1 %all-gather.6.cloned.1.call-done = bf16[8,64,1024]{2,1,0:T(8,128)(2,1)} async-done(((bf16[8,64,128]{2,1,0:T(8,128)(2,1)}), bf16[8,64,1024]{2,1,0:T(8,128)(2,1)}) %all-gather.6.cloned.1.call-update) | async-done | bytes 1048592 | tf_op jit(solution)/shard_map/all_gather | solution.py:34
  57.3 1.9 fusion.4
  59.1 28.3 %all_gather.15 = bf16[512,64]{1,0:T(8,128)(2,1)S(1)} all-gather(bf16[64,64]{1,0:T(8,128)(2,1)S(1)} %fusion.4), channel_id=1, replica_groups=mesh['dp'=64,'tensor'=8] {'tensor'}, dimensions={0}, use_global_device_ids=true | all-gather | bytes 73728 | tf_op jit(solution)/shard_map/all_gather | solution.py:71
  87.4 18.4 %all-gather.8.cloned.1.call-done = bf16[512,1024]{1,0:T(8,128)(2,1)} async-done(((bf16[64,1024]{1,0:T(8,128)(2,1)}), bf16[512,1024]{1,0:T(8,128)(2,1)}) %all-gather.8.cloned.1.call-update) | async-done | bytes 1048592 | tf_op jit(solution)/shard_map/all_gather | solution.py:70
  105.7 0.9 constant_dynamic-slice_fusion
  106.7 85.2 %all-reduce.4.cloned.1.call-done = bf16[4,128,64]{1,2,0:T(8,128)(2,1)} async-done(((bf16[4,128,64]{1,2,0:T(8,128)(2,1)}), bf16[4,128,64]{1,2,0:T(8,128)(2,1)}) %all-reduce.4.cloned.1.call-update) | async-done | bytes 65552 | tf_op jit(solution)/shard_map/psum | solution.py:41
  191.8 1.0 fusion.28
  192.8 1.1 fusion.9
  193.9 0.4 convolution_bitcast_fusion
  194.3 3.2 fusion.6
  197.5 0.0 all-reduce.6.cloned.1.call-update
  197.6 0.0 reduce-scatter.2.cloned.1.call-start
  197.6 81.2 %all-gather.4.cloned.1.call-done = bf16[1024,1024]{0,1:T(8,128)(2,1)} async-done(((bf16[1024,16]{0,1:T(8,128)(2,1)}), bf16[1024,1024]{0,1:T(8,128)(2,1)}) %all-gather.4.cloned.1.call-update) | async-done | bytes 2097168 | tf_op jit(solution)/shard_map/all_gather | solution.py:42
  278.9 3.9 convolution_convert_fusion
  282.7 0.0 reduce-scatter.2.cloned.1.call-update
  282.8 0.1 select_reduce_fusion
  282.9 0.1 constant_dynamic-slice_fusion.1
  283.0 0.1 copy.28
  283.1 0.4 convolution_multiply_fusion
  283.5 0.4 copy-done.5
  283.9 0.8 copy-done.8
  284.8 2.2 fusion
  287.0 548.4 %all-reduce.6.cloned.1.call-done = (f32[8,1024,64]{1,0,2:T(8,128)}, f32[8,64,128]{2,0,1:T(8,128)}) async-done(((f32[8,1024,64]{1,0,2:T(8,128)}, f32[8,64,128]{2,0,1:T(8,128)}), (f32[8,1024,64]{1,0,2:T(8,128)}, f32[8,64,128]{2,0,1:T(8,128)})) %all-reduce.6.cloned.1.call-update) | async-done | bytes 2359312 | tf_op jit(solution)/shard_map/psum | solution.py:93
  835.4 1.8 broadcast_multiply_fusion
  837.3 2.5 copy.34
  839.8 0.1 broadcast_multiply_fusion.1
  839.9 0.8 copy.35
  840.7 41.4 %reduce-scatter.2.cloned.1.call-done = bf16[64,1024]{1,0:T(8,128)(2,1)} async-done(((bf16[512,1024]{1,0:T(8,128)(2,1)}), bf16[64,1024]{1,0:T(8,128)(2,1)}) %reduce-scatter.2.cloned.1.call-update) | async-done | bytes 131088 | tf_op jit(solution)/shard_map/reduce_scatter | solution.py:43
  882.1 2.0 fusion.3
  (20 shorter events, 0.1 us)
Async XLA Ops:
  7.2 9.0 %copy-start = (bf16[512,1024]{1,0:T(8,128)(2,1)S(1)}, bf16[512,1024]{1,0:T(8,128)(2,1)}, u32[]{:S(2)}) copy-start(bf16[512,1024]{1,0:T(8,128)(2,1)} %param.7) | copy-start | bytes 3145732
  7.2 50.1 %all-gather.6.cloned.1.call-start = ((), (), s32[]{:S(2)}) async-start(), calls=%async_computation.4 | async-start | bytes 1179648 | tf_op jit(solution)/shard_map/all_gather | solution.py:34
  7.9 97.8 %all-gather.8.cloned.1.call-start = ((), (), s32[]{:S(2)}) async-start(), calls=%async_computation.5 | async-start | bytes 1179648 | tf_op jit(solution)/shard_map/all_gather | solution.py:70
  13.6 43.7 %copy-start.2 = (bf16[64,1024]{1,0:T(8,128)(2,1)S(1)}, bf16[64,1024]{1,0:T(8,128)(2,1)}, u32[]{:S(2)}) copy-start(bf16[64,1024]{1,0:T(8,128)(2,1)} %broadcast_select_fusion) | copy-start | bytes 393220
  13.6 178.2 %all-reduce.4.cloned.1.call-start = ((), (), s32[]{:S(2)}) async-start(), calls=%async_computation.3 | async-start | bytes 131072 | tf_op jit(solution)/shard_map/psum | solution.py:41
  17.3 261.5 %all-gather.4.cloned.1.call-start = ((), (), s32[]{:S(2)}) async-start(), calls=%async_computation.1 | async-start | bytes 2129920 | tf_op jit(solution)/shard_map/all_gather | solution.py:42
  17.9 817.5 %all-reduce.6.cloned.1.call-start = ((), (), s32[]{:S(2)}) async-start(), calls=%async_computation.6 | async-start | bytes 4718592 | tf_op jit(solution)/shard_map/psum | solution.py:93
  197.5 85.2 %copy-start.7 = (s32[256]{0:T(256)S(1)}, s32[256]{0:T(256)}, u32[]{:S(2)}) copy-start(s32[256]{0:T(256)} %param.13) | copy-start | bytes 3076
  197.5 85.2 %copy-start.6 = (s32[256,1]{0,1:T(1,128)S(1)}, s32[256,1]{0,1:T(1,128)}, u32[]{:S(2)}) copy-start(s32[256,1]{0,1:T(1,128)} %param.12) | copy-start | bytes 3076
  197.6 85.4 %copy-start.4 = (bf16[4,128,64]{1,2,0:T(8,128)(2,1)S(1)}, bf16[4,128,64]{1,2,0:T(8,128)(2,1)}, u32[]{:S(2)}) copy-start(bf16[4,128,64]{1,2,0:T(8,128)(2,1)} %all-reduce.4.cloned.1.call-done) | copy-start | bytes 196612
  197.6 684.5 %reduce-scatter.2.cloned.1.call-start = ((), (), s32[]{:S(2)}) async-start(), calls=%async_computation.2 | async-start | bytes 1179648 | tf_op jit(solution)/shard_map/reduce_scatter | solution.py:43
  282.7 1.2 copy-start.5
  283.1 1.7 copy-start.8
  837.3 2.6 copy-start.3
  837.3 44.8 %copy-start.1 = (bf16[8,64,1024]{2,1,0:T(8,128)(2,1)S(1)}, bf16[8,64,1024]{2,1,0:T(8,128)(2,1)}, u32[]{:S(2)}) copy-start(bf16[8,64,1024]{2,1,0:T(8,128)(2,1)} %all-gather.6.cloned.1.call-done) | copy-start | bytes 3145732
Sparse Core Ops, SparseCore 0:
  10.0 47.1 all-gather.5
  59.9 45.7 all-gather.7
  109.2 82.5 all-reduce.3
  195.6 83.2 all-gather.3
  282.5 552.8 all-reduce.5
  838.1 43.9 reduce-scatter.1
where the time goes:
time: 891 us
  waiting for transfers between devices  812 us (91%)
  blocking collectives  28.3 us (3%)
  matrix products  17.1 us (2%)
  between operations  14.3 us (2%)
  other arithmetic  9.62 us (1%)
  local copies, waits for them, and re-layouts  9.44 us (1%)
    psum x1, waiting for transfers between devices, shards(): down_sum, up_sum = lax.psum((down_local, up_local), 'dp')  548 us
    psum x1, waiting for transfers between devices, shards(): reduced = lax.psum(reduced_part.astype(jnp.bfloat16), 'tensor')  85.2 us
    all_gather x1, waiting for transfers between devices, shards(): w_full = lax.all_gather(value_weight, 'dp', axis=1, tiled=True)  81.2 us
    reduce_scatter x1, waiting for transfers between devices, shards(): lax.psum_scatter(jnp.dot(tokens, w_full, preferred_element_type=jnp.float...  41.4 us
    all_gather x1, waiting for transfers between devices, shards(): lax.all_gather(adapter_up_weights, 'tensor', axis=2, tiled=True)  36.1 us
    all_gather x1, blocking collectives, shards(): lax.all_gather(grad_low, 'tensor', axis=0, tiled=True)  28.3 us
    all_gather x1, waiting for transfers between devices, shards(): lax.all_gather(masked, 'tensor', axis=0, tiled=True)  18.4 us
  transfers between devices with their start and end apart: 6, of which 6 were waited for; matrix products, arithmetic and copies ran while one was open for 4% of the time, Pallas kernels for 0%

commit v1 on v0

--- a/solution.py
+++ b/solution.py
@@ -38,7 +38,8 @@
     reduced_part = jnp.einsum(
         "cpe,cev->cpv", token_block_rows, selected_down_weight, preferred_element_type=jnp.float32
     )
-    reduced = lax.psum(reduced_part.astype(jnp.bfloat16), "tensor")
+    inputs = reduced_part.astype(jnp.bfloat16)
+    reduced = lax.all_gather(inputs, axis_name="tensor").sum(axis=0)
     w_full = lax.all_gather(value_weight, "dp", axis=1, tiled=True)
     base_own = lax.psum_scatter(
         jnp.dot(tokens, w_full, preferred_element_type=jnp.float32).astype(jnp.bfloat16),

time: 891 us -> 806 us (0.905)
  waiting for transfers between devices: 812 us -> 697 us
  blocking collectives: 28.3 us -> 59.3 us
    psum x1 -> x0, waiting for transfers between devices: 85.2 us -> none  [shards(): reduced = lax.psum(reduced_part.astype(jnp.bfloat16), 'tensor')]
    all_gather x0 -> x1, blocking collectives: none -> 30.8 us  [shards(): reduced = lax.all_gather(inputs, axis_name='tensor').sum(axis=0)]
    all_gather x1, waiting for transfers between devices: 36.1 us -> 6.64 us  [shards(): lax.all_gather(adapter_up_weights, 'tensor', axis=2, tiled=True)]
  transfers between devices with their start and end apart: 6 -> 5, of which waited for: 6 -> 5; matrix products, arithmetic and copies ran while one was open for 4% -> 4% of each run, Pallas kernels for 0% -> 0%
where the time goes in v1:
time: 806 us; the launch traced here: 805 us
  waiting for transfers between devices  697 us (86%)
  blocking collectives  59.3 us (7%)
  matrix products  15.7 us (2%)
  between operations  13.9 us (2%)
  other arithmetic  9.69 us (1%)
  local copies, waits for them, and re-layouts  9.37 us (1%)
    psum x1, waiting for transfers between devices, shards(): down_sum, up_sum = lax.psum((down_local, up_local), 'dp')  548 us
    all_gather x1, waiting for transfers between devices, shards(): w_full = lax.all_gather(value_weight, 'dp', axis=1, tiled=True)  80.6 us
    reduce_scatter x1, waiting for transfers between devices, shards(): lax.psum_scatter(jnp.dot(tokens, w_full, preferred_element_type=jnp.float...  41.6 us
    all_gather x1, blocking collectives, shards(): reduced = lax.all_gather(inputs, axis_name='tensor').sum(axis=0)  30.8 us
    all_gather x1, blocking collectives, shards(): lax.all_gather(grad_low, 'tensor', axis=0, tiled=True)  28.5 us
    all_gather x1, waiting for transfers between devices, shards(): lax.all_gather(masked, 'tensor', axis=0, tiled=True)  18.5 us
  transfers between devices with their start and end apart: 5, of which 5 were waited for; matrix products, arithmetic and copies ran while one was open for 4% of the time, Pallas kernels for 0%

profile of v1, /device:TPU:8, one launch (start us, length us, event | category | flops | bytes accessed | tf_op | source)
XLA Modules:
  0.0 805.2 jit_solution(5225676751857999779)
XLA Ops:
  7.2 0.0 copy-start
  7.2 0.0 all-gather.7.cloned.1.call-start
  7.2 0.7 all-gather.7.cloned.1.call-update
  7.9 0.0 all-gather.9.cloned.1.call-start
  8.0 0.8 dynamic_slice.17
  8.7 0.6 fusion.26
  9.3 2.6 fusion.21
  11.9 1.6 broadcast_select_fusion
  13.6 0.0 all-gather.9.cloned.1.call-update
  13.6 0.0 all-gather.5.cloned.1.call-start
  13.6 0.7 all-gather.5.cloned.1.call-update
  14.3 0.0 all-reduce.3.cloned.1.call-start
  14.4 0.7 fusion.25
  15.1 1.8 gather_fusion
  17.0 0.5 fusion.5
  17.5 30.8 %all-gather = bf16[32,128,64]{1,2,0:T(8,128)(2,1)S(1)} all-gather(bf16[4,128,64]{1,2,0:T(8,128)(2,1)S(1)} %fusion.5), channel_id=2, replica_groups=mesh['dp'=64,'tensor'=8] {'tensor'}, dimensions={0}, use_global_device_ids=true | all-gather | bytes 589824 | tf_op jit(solution)/shard_map/all_gather | solution.py:42
  48.3 0.1 reduce_sum.30
  48.4 0.6 fusion.27
  49.0 2.6 fusion.23
  51.5 6.6 all-gather.7.cloned.1.call-done
  58.2 1.9 fusion.4
  60.0 28.5 %all_gather.23 = bf16[512,64]{1,0:T(8,128)(2,1)S(1)} all-gather(bf16[64,64]{1,0:T(8,128)(2,1)S(1)} %fusion.4), channel_id=1, replica_groups=mesh['dp'=64,'tensor'=8] {'tensor'}, dimensions={0}, use_global_device_ids=true | all-gather | bytes 73728 | tf_op jit(solution)/shard_map/all_gather | solution.py:72
  88.5 18.5 %all-gather.9.cloned.1.call-done = bf16[512,1024]{1,0:T(8,128)(2,1)} async-done(((bf16[64,1024]{1,0:T(8,128)(2,1)}), bf16[512,1024]{1,0:T(8,128)(2,1)}) %all-gather.9.cloned.1.call-update) | async-done | bytes 1048592 | tf_op jit(solution)/shard_map/all_gather | solution.py:71
  107.1 0.9 constant_dynamic-slice_fusion
  108.0 0.1 fusion.28
  108.1 1.1 fusion.9
  109.3 0.3 convolution_bitcast_fusion
  109.6 3.2 fusion.6
  112.8 0.0 all-reduce.3.cloned.1.call-update
  112.8 0.0 copy-start.6
  112.9 0.0 reduce-scatter.2.cloned.1.call-start
  112.9 80.6 %all-gather.5.cloned.1.call-done = bf16[1024,1024]{0,1:T(8,128)(2,1)} async-done(((bf16[1024,16]{0,1:T(8,128)(2,1)}), bf16[1024,1024]{0,1:T(8,128)(2,1)}) %all-gather.5.cloned.1.call-update) | async-done | bytes 2097168 | tf_op jit(solution)/shard_map/all_gather | solution.py:43
  193.5 3.9 convolution_convert_fusion
  197.4 0.0 reduce-scatter.2.cloned.1.call-update
  197.5 0.1 constant_dynamic-slice_fusion.1
  197.6 0.1 copy.33
  197.7 0.1 select_reduce_fusion
  197.8 0.4 convolution_multiply_fusion
  198.2 0.4 copy-done.4
  198.6 0.8 copy-done.7
  199.4 2.2 fusion
  201.6 548.2 %all-reduce.3.cloned.1.call-done = (f32[8,1024,64]{1,0,2:T(8,128)}, f32[8,64,128]{2,0,1:T(8,128)}) async-done(((f32[8,1024,64]{1,0,2:T(8,128)}, f32[8,64,128]{2,0,1:T(8,128)}), (f32[8,1024,64]{1,0,2:T(8,128)}, f32[8,64,128]{2,0,1:T(8,128)})) %all-reduce.3.cloned.1.call-update) | async-done | bytes 2359312 | tf_op jit(solution)/shard_map/psum | solution.py:94
  749.8 1.8 broadcast_multiply_fusion
  751.7 2.5 copy.39
  754.2 0.1 broadcast_multiply_fusion.1
  754.3 0.8 copy.40
  755.1 41.6 %reduce-scatter.2.cloned.1.call-done = bf16[64,1024]{1,0:T(8,128)(2,1)} async-done(((bf16[512,1024]{1,0:T(8,128)(2,1)}), bf16[64,1024]{1,0:T(8,128)(2,1)}) %reduce-scatter.2.cloned.1.call-update) | async-done | bytes 131088 | tf_op jit(solution)/shard_map/reduce_scatter | solution.py:44
  796.7 2.0 fusion.3
  (17 shorter events, 0.1 us)
Async XLA Ops:
  7.2 9.8 %copy-start = (bf16[512,1024]{1,0:T(8,128)(2,1)S(1)}, bf16[512,1024]{1,0:T(8,128)(2,1)}, u32[]{:S(2)}) copy-start(bf16[512,1024]{1,0:T(8,128)(2,1)} %param.7) | copy-start | bytes 3145732
  7.2 51.0 %all-gather.7.cloned.1.call-start = ((), (), s32[]{:S(2)}) async-start(), calls=%async_computation.3 | async-start | bytes 1179648 | tf_op jit(solution)/shard_map/all_gather | solution.py:34
  7.9 99.1 %all-gather.9.cloned.1.call-start = ((), (), s32[]{:S(2)}) async-start(), calls=%async_computation.4 | async-start | bytes 1179648 | tf_op jit(solution)/shard_map/all_gather | solution.py:71
  13.6 179.9 %all-gather.5.cloned.1.call-start = ((), (), s32[]{:S(2)}) async-start(), calls=%async_computation.1 | async-start | bytes 2129920 | tf_op jit(solution)/shard_map/all_gather | solution.py:43
  14.3 735.5 %all-reduce.3.cloned.1.call-start = ((), (), s32[]{:S(2)}) async-start(), calls=%async_computation.5 | async-start | bytes 4718592 | tf_op jit(solution)/shard_map/psum | solution.py:94
  15.1 43.1 %copy-start.2 = (bf16[64,1024]{1,0:T(8,128)(2,1)S(1)}, bf16[64,1024]{1,0:T(8,128)(2,1)}, u32[]{:S(2)}) copy-start(bf16[64,1024]{1,0:T(8,128)(2,1)} %broadcast_select_fusion) | copy-start | bytes 393220
  112.8 84.6 %copy-start.6 = (s32[256]{0:T(256)S(1)}, s32[256]{0:T(256)}, u32[]{:S(2)}) copy-start(s32[256]{0:T(256)} %param.13) | copy-start | bytes 3076
  112.9 84.8 %copy-start.5 = (s32[256,1]{0,1:T(1,128)S(1)}, s32[256,1]{0,1:T(1,128)}, u32[]{:S(2)}) copy-start(s32[256,1]{0,1:T(1,128)} %param.12) | copy-start | bytes 3076
  112.9 683.8 %reduce-scatter.2.cloned.1.call-start = ((), (), s32[]{:S(2)}) async-start(), calls=%async_computation.2 | async-start | bytes 1179648 | tf_op jit(solution)/shard_map/reduce_scatter | solution.py:44
  197.4 1.2 copy-start.4
  197.7 1.7 copy-start.7
  751.7 2.6 copy-start.3
  751.7 45.0 %copy-start.1 = (bf16[8,64,1024]{2,1,0:T(8,128)(2,1)S(1)}, bf16[8,64,1024]{2,1,0:T(8,128)(2,1)}, u32[]{:S(2)}) copy-start(bf16[8,64,1024]{2,1,0:T(8,128)(2,1)} %all-gather.7.cloned.1.call-done) | copy-start | bytes 3145732
Sparse Core Ops, SparseCore 0:
  10.0 48.1 all-gather.6
  60.8 46.1 all-gather.8
  110.4 83.0 all-gather.4
  197.0 552.8 all-reduce.2
  752.7 43.9 reduce-scatter.1
